TPU v7x, 32 devices: a whole 2x2x4 slice. The times are simulated.
32 devices in a mesh: blk: 8 (over y, x, core), head: 4 (over z).
Axes of the slice: x: 2, y: 2, z: 4, core: 2. Of those that a mesh axis runs over, the one named last changes fastest.
Arguments:
- qkv: bfloat16 [4096, 8, 768], P(('blk', 'head')), may hold values from -40 to 40, as said below
- lambda_params: float32 [4, 128], replicated, may hold values from -0.4 to 0.4
- norm_gain: float32 [256], replicated, may hold values from 0.5 to 1.5
Outputs:
- mixed: bfloat16 [4096, 2048], P(('blk', 'head'))
Inputs may be any that keep to these rules, and one draw needn't show every extreme that they name: `qkv`: entries of order one, some larger.
All inputs are finite; a program needn't handle non-finite values.
Results may differ from a plain program's by a relative error of at most 0.006.
Values may be sent and summed in bfloat16 or wider, within the bound.
A program may use at most 192 MiB of HBM per device.

v0:
```python
import math

import jax
import jax.numpy as jnp
from jax import lax
from jax.sharding import PartitionSpec as P

lambda_init = 0.2
far_below = -1e30


def positions(stored, count_blk, block_rows):
    half_rows = block_rows // 2
    owner = stored // block_rows
    within = stored % block_rows
    return jnp.where(
        within < half_rows,
        owner * half_rows + within,
        (2 * count_blk - 1 - owner) * half_rows + within - half_rows,
    )


def update(states, queries, key_map, values, query_pos, key_pos, score_scale):
    maxima, totals, running = states
    scores = (
        jnp.einsum("qhd,khd->hqk", queries, key_map, preferred_element_type=jnp.float32)
        * score_scale
    )
    visible = (key_pos[None, :] <= query_pos[:, None])[None, :, :]
    row_top = jnp.max(jnp.where(visible, scores, far_below), axis=2)
    new_max = jnp.maximum(maxima, row_top)
    weights = jnp.where(visible, jnp.exp(scores - new_max[:, :, None]), 0.0)
    factor = jnp.exp(maxima - new_max)
    totals = totals * factor + jnp.sum(weights, axis=2)
    running = running * factor[:, :, None] + jnp.einsum(
        "hqk,khe->hqe", weights.astype(jnp.bfloat16), values, preferred_element_type=jnp.float32
    )
    return (new_max, totals, running)


def update_all(all_states, query_maps, key_maps, values, query_pos, key_pos, score_scale):
    return tuple(
        (
            update(state_one, query_map, key_map, values, query_pos, key_pos, score_scale)
            for state_one, query_map, key_map in zip(all_states, query_maps, key_maps)
        )
    )


def sweep_keys(all_states, query_maps, key_maps, values, query_pos, count_blk):
    block_rows = query_pos.shape[0]
    key_count = values.shape[0]
    block_size = key_count
    while block_size > 2048 and block_size % 2 == 0:
        block_size = block_size // 2
    block_count = key_count // block_size
    score_scale = 1.0 / math.sqrt(query_maps[0].shape[2])
    key_pos = positions(jnp.arange(key_count, dtype=jnp.int32), count_blk, block_rows)
    blocks = (
        tuple(
            (
                key_map.reshape(block_count, block_size, key_map.shape[1], key_map.shape[2])
                for key_map in key_maps
            )
        ),
        values.reshape(block_count, block_size, values.shape[1], values.shape[2]),
        key_pos.reshape(block_count, block_size),
    )

    def advance(carry, block):
        key_blocks, value_block, pos_block = block
        return (
            update_all(
                carry, query_maps, key_blocks, value_block, query_pos, pos_block, score_scale
            ),
            None,
        )

    all_states, unused = lax.scan(advance, all_states, blocks)
    return all_states


def local(qkv, lambda_params, norm_gain):
    count_blk = lax.axis_size("blk")
    key_width = lambda_params.shape[1]
    value_width = norm_gain.shape[0]
    regrouped = lax.all_to_all(qkv, "head", split_axis=1, concat_axis=0, tiled=True)
    block_rows = regrouped.shape[0]
    heads_here = regrouped.shape[1]
    query_one = regrouped[:, :, 0:key_width]
    query_two = regrouped[:, :, key_width : 2 * key_width]
    query_pos = positions(
        lax.axis_index("blk") * block_rows + jnp.arange(block_rows, dtype=jnp.int32),
        count_blk,
        block_rows,
    )
    initial = (
        jnp.full((heads_here, block_rows), far_below, jnp.float32),
        jnp.zeros((heads_here, block_rows), jnp.float32),
        jnp.zeros((heads_here, block_rows, value_width), jnp.float32),
    )
    pieces = lax.all_gather(regrouped[:, :, 2 * key_width :], "blk", axis=0, tiled=True)
    key_one = pieces[:, :, 0:key_width]
    key_two = pieces[:, :, key_width : 2 * key_width]
    values_all = pieces[:, :, 2 * key_width :]
    first_state = sweep_keys(
        (initial,), (query_one,), (key_one,), values_all, query_pos, count_blk
    )[0]
    second_state = sweep_keys(
        (initial,), (query_two,), (key_two,), values_all, query_pos, count_blk
    )[0]
    lam_value = (
        jnp.exp(jnp.sum(lambda_params[0] * lambda_params[1]))
        - jnp.exp(jnp.sum(lambda_params[2] * lambda_params[3]))
        + lambda_init
    )
    out_one = first_state[2] / first_state[1][:, :, None]
    out_two = second_state[2] / second_state[1][:, :, None]
    difference = out_one - lam_value * out_two
    mean_square = jnp.mean(difference * difference, axis=2, keepdims=True)
    normed = difference * lax.rsqrt(mean_square + 1e-05) * norm_gain * (1.0 - lambda_init)
    returned = lax.all_to_all(
        normed.astype(jnp.bfloat16), "head", split_axis=1, concat_axis=0, tiled=True
    )
    return jnp.transpose(returned, (1, 0, 2)).reshape(
        returned.shape[1], returned.shape[0] * value_width
    )


def solution(mesh):
    return jax.shard_map(
        local,
        mesh=mesh,
        in_specs=(P(("blk", "head"), None, None), P(), P()),
        out_specs=P(("blk", "head"), None),
        check_vma=False,
    )
```

profile of v0, /device:TPU:0, one launch (start us, length us, event | category | flops | bytes accessed | tf_op | source)
XLA Modules:
  0.0 219.9 jit_solution(363369701973176632)
XLA Ops:
  6.5 1.7 copy.59
  8.3 43.1 %all_to_all.36 = bf16[128,8,768]{2,0,1:T(8,128)(2,1)S(1)} all-to-all(bf16[128,8,768]{2,0,1:T(8,128)(2,1)S(1)} %copy.59), channel_id=1, replica_groups=mesh['blk'=8,'head'=4] {'head'}, dimensions={1} | all-to-all | bytes 3145728 | tf_op jit(solution)/shard_map/all_to_all | solution.py:87
  55.5 50.8 %all-gather.2.cloned.1.call-done = bf16[4096,2,512]{2,0,1:T(8,128)(2,1)} async-done(((bf16[512,2,512]{2,0,1:T(8,128)(2,1)}), bf16[4096,2,512]{2,0,1:T(8,128)(2,1)}) %all-gather.2.cloned.1.call-update) | async-done | bytes 8388624 | tf_op jit(solution)/shard_map/all_gather | solution.py:102
  106.3 2.2 slice-done
  108.5 2.4 %copy.62 = bf16[2,2048,2,256]{3,1,2,0:T(8,128)(2,1)} copy(bf16[2,2048,2,256]{3,1,0,2:T(8,128)(2,1)S(1)} %bitcast.102) | data formatting | bytes 8388608
  110.9 1.6 copy-done.2
  112.5 2.0 fusion.62
  114.5 38.7 %while.30 = (s32[]{:T(128)}, f32[2,512]{1,0:T(2,128)S(1)}, f32[2,512]{1,0:T(2,128)S(1)}, f32[2,512,256]{2,1,0:T(8,128)}, s32[2,2048]{1,0:T(2,128)S(1)}, /*index=...) while((s32[]{:T(128)}, f32[2,512]{1,0:T(2,128)S(1)}, ...), condition=%wide.region_3.4_spmd.clone, body=%wide.region_0.3_spmd.clone.sunk | while | flops 1635535872 | bytes 76903640 | solution.py:79
  115.3 6.3 %fusion.85 = (f32[2,512]{1,0:T(2,128)S(1)}, f32[2,2048,512]{2,1,0:T(8,128)}) fusion(pred[512,2048]{0,1:T(8,128)(4,1)S(1)} %broadcast_compare_fusion.4, bf16[512,2,128]{2,0,1:T(8,128)(2,1)} %get-tuple-element.509, bf16[2,2048,2,128]{3,1,0,2:T(8,128)(2,1)} %get-tuple-element.508, s32[]{:T(128)} %get-tuple-element.492), kind=kOutput, calls=%fused_computation.4.clone.1 | convolution fusion | flops 543161344 | bytes 10752512 | tf_op jit(solution)/shard_map/while/body/eval_jaxpr/qhd,khd->hqk/dot_general | solution.py:26
  121.6 4.6 %fusion.87 = f32[2,512]{1,0:T(2,128)S(1)} fusion(f32[2,2048,512]{2,1,0:T(8,128)} %get-tuple-element.432, f32[2,512]{1,0:T(2,128)S(1)} %fusion.86, pred[512,2048]{0,1:T(8,128)(4,1)S(1)} %broadcast_compare_fusion.4), kind=kLoop, calls=%fused_computation.8.clone.1 | loop fusion | flops 8387584 | bytes 9445376 | tf_op jit(solution)/shard_map/while/body/eval_jaxpr/reduce_sum | solution.py:34
  127.7 5.2 %fusion.89 = f32[2,512,256]{2,1,0:T(8,128)S(1)} fusion(bf16[2,2048,2,256]{3,1,2,0:T(8,128)(2,1)} %get-tuple-element.510, s32[]{:T(128)} %get-tuple-element.492, f32[2,2048,512]{2,1,0:T(8,128)S(1)} %copy-done, f32[2,512]{1,0:T(2,128)S(1)} %fusion.86, pred[512,2048]{0,1:T(8,128)(4,1)S(1)} %broadcast_compare_fusion.4, ...), kind=kOutput, calls=%fused_computation.17.clone.1 | convolution fusion | flops 1082916864 | bytes 13640193 | tf_op jit(solution)/shard_map/while/body/eval_jaxpr/hqk,khe->hqe/dot_general | solution.py:35
  134.7 6.3 %fusion.85 = (f32[2,512]{1,0:T(2,128)S(1)}, f32[2,2048,512]{2,1,0:T(8,128)}) fusion(pred[512,2048]{0,1:T(8,128)(4,1)S(1)} %broadcast_compare_fusion.4, bf16[512,2,128]{2,0,1:T(8,128)(2,1)} %get-tuple-element.509, bf16[2,2048,2,128]{3,1,0,2:T(8,128)(2,1)} %get-tuple-element.508, s32[]{:T(128)} %get-tuple-element.492), kind=kOutput, calls=%fused_computation.4.clone.1 | convolution fusion | flops 543161344 | bytes 10752512 | tf_op jit(solution)/shard_map/while/body/eval_jaxpr/qhd,khd->hqk/dot_general | solution.py:26
  141.0 4.6 %fusion.87 = f32[2,512]{1,0:T(2,128)S(1)} fusion(f32[2,2048,512]{2,1,0:T(8,128)} %get-tuple-element.432, f32[2,512]{1,0:T(2,128)S(1)} %fusion.86, pred[512,2048]{0,1:T(8,128)(4,1)S(1)} %broadcast_compare_fusion.4), kind=kLoop, calls=%fused_computation.8.clone.1 | loop fusion | flops 8387584 | bytes 9445376 | tf_op jit(solution)/shard_map/while/body/eval_jaxpr/reduce_sum | solution.py:34
  147.0 5.2 %fusion.89 = f32[2,512,256]{2,1,0:T(8,128)S(1)} fusion(bf16[2,2048,2,256]{3,1,2,0:T(8,128)(2,1)} %get-tuple-element.510, s32[]{:T(128)} %get-tuple-element.492, f32[2,2048,512]{2,1,0:T(8,128)S(1)} %copy-done, f32[2,512]{1,0:T(2,128)S(1)} %fusion.86, pred[512,2048]{0,1:T(8,128)(4,1)S(1)} %broadcast_compare_fusion.4, ...), kind=kOutput, calls=%fused_computation.17.clone.1 | convolution fusion | flops 1082916864 | bytes 13640193 | tf_op jit(solution)/shard_map/while/body/eval_jaxpr/hqk,khe->hqe/dot_general | solution.py:35
  153.2 36.2 %while.31 = (s32[]{:T(128)}, f32[2,512]{1,0:T(2,128)S(1)}, f32[2,512]{1,0:T(2,128)S(1)}, f32[2,512,256]{2,1,0:T(8,128)}, s32[2,2048]{1,0:T(2,128)S(1)}, /*index=...) while((s32[]{:T(128)}, f32[2,512]{1,0:T(2,128)S(1)}, ...), condition=%wide.region_9.10_spmd.clone, body=%wide.region_6.9_spmd.clone.sunk | while | flops 1635535872 | bytes 76903128 | solution.py:79
  154.1 5.0 %fusion.93 = (f32[2,512]{1,0:T(2,128)S(1)}, f32[2,2048,512]{2,1,0:T(8,128)}) fusion(pred[512,2048]{0,1:T(8,128)(4,1)S(1)} %broadcast_compare_fusion.5, bf16[512,2,128]{2,0,1:T(8,128)(2,1)S(1)} %get-tuple-element.476, bf16[2,2048,2,128]{3,1,0,2:T(8,128)(2,1)S(1)} %get-tuple-element.475, s32[]{:T(128)} %get-tuple-element.459), kind=kOutput, calls=%fused_computation.44.clone.1 | convolution fusion | flops 543161344 | bytes 10752004 | tf_op jit(solution)/shard_map/while/body/eval_jaxpr/qhd,khd->hqk/dot_general | solution.py:26
  159.1 4.6 %fusion.95 = f32[2,512]{1,0:T(2,128)S(1)} fusion(f32[2,2048,512]{2,1,0:T(8,128)} %get-tuple-element.445, f32[2,512]{1,0:T(2,128)S(1)} %fusion.94, pred[512,2048]{0,1:T(8,128)(4,1)S(1)} %broadcast_compare_fusion.5), kind=kLoop, calls=%fused_computation.48.clone.1 | loop fusion | flops 8387584 | bytes 9445376 | tf_op jit(solution)/shard_map/while/body/eval_jaxpr/reduce_sum | solution.py:34
  165.1 5.2 %fusion.97 = f32[2,512,256]{2,1,0:T(8,128)S(1)} fusion(bf16[2,2048,2,256]{3,1,2,0:T(8,128)(2,1)} %get-tuple-element.477, s32[]{:T(128)} %get-tuple-element.459, f32[2,2048,512]{2,1,0:T(8,128)S(1)} %copy-done.1, f32[2,512]{1,0:T(2,128)S(1)} %fusion.94, pred[512,2048]{0,1:T(8,128)(4,1)S(1)} %broadcast_compare_fusion.5, ...), kind=kOutput, calls=%fused_computation.57.clone.1 | convolution fusion | flops 1082916864 | bytes 13640193 | tf_op jit(solution)/shard_map/while/body/eval_jaxpr/hqk,khe->hqe/dot_general | solution.py:35
  172.2 5.0 %fusion.93 = (f32[2,512]{1,0:T(2,128)S(1)}, f32[2,2048,512]{2,1,0:T(8,128)}) fusion(pred[512,2048]{0,1:T(8,128)(4,1)S(1)} %broadcast_compare_fusion.5, bf16[512,2,128]{2,0,1:T(8,128)(2,1)S(1)} %get-tuple-element.476, bf16[2,2048,2,128]{3,1,0,2:T(8,128)(2,1)S(1)} %get-tuple-element.475, s32[]{:T(128)} %get-tuple-element.459), kind=kOutput, calls=%fused_computation.44.clone.1 | convolution fusion | flops 543161344 | bytes 10752004 | tf_op jit(solution)/shard_map/while/body/eval_jaxpr/qhd,khd->hqk/dot_general | solution.py:26
  177.2 4.6 %fusion.95 = f32[2,512]{1,0:T(2,128)S(1)} fusion(f32[2,2048,512]{2,1,0:T(8,128)} %get-tuple-element.445, f32[2,512]{1,0:T(2,128)S(1)} %fusion.94, pred[512,2048]{0,1:T(8,128)(4,1)S(1)} %broadcast_compare_fusion.5), kind=kLoop, calls=%fused_computation.48.clone.1 | loop fusion | flops 8387584 | bytes 9445376 | tf_op jit(solution)/shard_map/while/body/eval_jaxpr/reduce_sum | solution.py:34
  181.8 1.2 copy-done.1
  183.3 5.2 %fusion.97 = f32[2,512,256]{2,1,0:T(8,128)S(1)} fusion(bf16[2,2048,2,256]{3,1,2,0:T(8,128)(2,1)} %get-tuple-element.477, s32[]{:T(128)} %get-tuple-element.459, f32[2,2048,512]{2,1,0:T(8,128)S(1)} %copy-done.1, f32[2,512]{1,0:T(2,128)S(1)} %fusion.94, pred[512,2048]{0,1:T(8,128)(4,1)S(1)} %broadcast_compare_fusion.5, ...), kind=kOutput, calls=%fused_computation.57.clone.1 | convolution fusion | flops 1082916864 | bytes 13640193 | tf_op jit(solution)/shard_map/while/body/eval_jaxpr/hqk,khe->hqe/dot_general | solution.py:35
  189.5 2.0 multiply_reduce_fusion
  192.3 19.3 %all_to_all.37 = bf16[2,512,256]{2,0,1:T(2,128)(2,1)S(1)} all-to-all(bf16[2,512,256]{2,0,1:T(2,128)(2,1)S(1)} %copy.65), channel_id=1, replica_groups=mesh['blk'=8,'head'=4] {'head'}, dimensions={1} | all-to-all | bytes 1048576 | tf_op jit(solution)/shard_map/all_to_all | solution.py:122
  (73 shorter events, 16.7 us)
Async XLA Ops:
  6.5 46.1 %copy-start.7 = (f32[4,128]{1,0:T(4,128)S(1)}, f32[4,128]{1,0:T(4,128)}, u32[]{:S(2)}) copy-start(f32[4,128]{1,0:T(4,128)} %param.8) | copy-start | bytes 6148
  6.5 99.8 %all-gather.2.cloned.1.call-start = ((), (), s32[]{:S(2)}) async-start(), calls=%async_computation.2 | async-start | bytes 9437184 | tf_op jit(solution)/shard_map/all_gather | solution.py:102
  106.3 2.2 slice-start
  106.3 6.2 %copy-start.2 = (bf16[4096,2,512]{2,0,1:T(8,128)(2,1)S(1)}, bf16[4096,2,512]{2,0,1:T(8,128)(2,1)}, u32[]{:S(2)}) copy-start(bf16[4096,2,512]{2,0,1:T(8,128)(2,1)} %all-gather.2.cloned.1.call-done) | copy-start | bytes 25165828
  121.6 5.8 %copy-start = (f32[2,2048,512]{2,1,0:T(8,128)S(1)}, f32[2,2048,512]{2,1,0:T(8,128)}, u32[]{:S(2)}) copy-start(f32[2,2048,512]{2,1,0:T(8,128)} %get-tuple-element.432) | copy-start | bytes 25165828 | tf_op jit(solution)/shard_map/while
  121.6 6.1 %copy-start.5 = (f32[2,512,256]{2,1,0:T(8,128)S(1)}, f32[2,512,256]{2,1,0:T(8,128)}, u32[]{:S(2)}) copy-start(f32[2,512,256]{2,1,0:T(8,128)} %get-tuple-element.495) | copy-start | bytes 3145732 | tf_op jit(solution)/shard_map/while
  132.9 1.0 copy-start.6
  141.0 5.8 %copy-start = (f32[2,2048,512]{2,1,0:T(8,128)S(1)}, f32[2,2048,512]{2,1,0:T(8,128)}, u32[]{:S(2)}) copy-start(f32[2,2048,512]{2,1,0:T(8,128)} %get-tuple-element.432) | copy-start | bytes 25165828 | tf_op jit(solution)/shard_map/while
  141.0 6.1 %copy-start.5 = (f32[2,512,256]{2,1,0:T(8,128)S(1)}, f32[2,512,256]{2,1,0:T(8,128)}, u32[]{:S(2)}) copy-start(f32[2,512,256]{2,1,0:T(8,128)} %get-tuple-element.495) | copy-start | bytes 3145732 | tf_op jit(solution)/shard_map/while
  152.3 1.0 copy-start.6
  153.2 38.3 %copy-start.8 = (f32[256]{0:T(256)S(1)}, f32[256]{0:T(256)}, u32[]{:S(2)}) copy-start(f32[256]{0:T(256)} %param.9) | copy-start | bytes 3076
  159.1 5.8 %copy-start.1 = (f32[2,2048,512]{2,1,0:T(8,128)S(1)}, f32[2,2048,512]{2,1,0:T(8,128)}, u32[]{:S(2)}) copy-start(f32[2,2048,512]{2,1,0:T(8,128)} %get-tuple-element.445) | copy-start | bytes 25165828 | tf_op jit(solution)/shard_map/while
  159.1 6.1 %copy-start.3 = (f32[2,512,256]{2,1,0:T(8,128)S(1)}, f32[2,512,256]{2,1,0:T(8,128)}, u32[]{:S(2)}) copy-start(f32[2,512,256]{2,1,0:T(8,128)} %get-tuple-element.462) | copy-start | bytes 3145732 | tf_op jit(solution)/shard_map/while
  170.4 1.0 copy-start.4
  177.2 5.8 %copy-start.1 = (f32[2,2048,512]{2,1,0:T(8,128)S(1)}, f32[2,2048,512]{2,1,0:T(8,128)}, u32[]{:S(2)}) copy-start(f32[2,2048,512]{2,1,0:T(8,128)} %get-tuple-element.445) | copy-start | bytes 25165828 | tf_op jit(solution)/shard_map/while
  177.2 6.1 %copy-start.3 = (f32[2,512,256]{2,1,0:T(8,128)S(1)}, f32[2,512,256]{2,1,0:T(8,128)}, u32[]{:S(2)}) copy-start(f32[2,512,256]{2,1,0:T(8,128)} %get-tuple-element.462) | copy-start | bytes 3145732 | tf_op jit(solution)/shard_map/while
  188.5 1.0 copy-start.4
Sparse Core Ops, SparseCore 0:
  52.7 53.5 all-gather.1
where the time goes:
time: 220 us
  blocking collectives  62.4 us (28%)
  waiting for transfers between devices  50.8 us (23%)
  matrix products  43.5 us (20%)
  other arithmetic  24.5 us (11%)
  local copies, waits for them, and re-layouts  23.7 us (11%)
  between operations  14.9 us (7%)
    all_gather x1, waiting for transfers between devices, local(): lax.all_gather(regrouped[:, :, 2 * key_width:], 'blk', axis=0, tiled=True)  50.8 us
    all_to_all x1, blocking collectives, local(): lax.all_to_all(qkv, 'head', split_axis=1, concat_axis=0, tiled=True)  43.1 us
    dot_general x4, matrix products, update(): jnp.einsum('qhd,khd->hqk', queries, key_map, preferred_element_type=jnp.f...  22.6 us
    dot_general x4, matrix products, update(): jnp.einsum('hqk,khe->hqe', weights.astype(jnp.bfloat16), values, preferre...  20.9 us
    all_to_all x1, blocking collectives, local(): lax.all_to_all(normed.astype(jnp.bfloat16), 'head', split_axis=1, concat_...  19.3 us
    reduce_sum x4, other arithmetic, update(): totals = totals * factor + jnp.sum(weights, axis=2)  18.3 us
    while x28, local copies, waits for them, and re-layouts  9.75 us
    unnamed x8, local copies, waits for them, and re-layouts  5.7 us
  transfers between devices with their start and end apart: 1, of which 1 were waited for; matrix products, arithmetic and copies ran while one was open for 1% of the time, Pallas kernels for 0%

commit v1 on v0

v1 whole, which is shorter than its diff:
```python
import functools
import math

import jax
import jax.numpy as jnp
from jax import lax
from jax.experimental import pallas as pl
from jax.experimental.pallas import tpu as pltpu
from jax.sharding import PartitionSpec as P

lambda_init = 0.2
far_below = -1e30
MESH = pl.DeviceIdType.MESH


def flip(index, code):
    out = index
    bit = 1
    while bit <= code:
        if code & bit:
            out = out + (1 - 2 * ((index // bit) % 2)) * bit
        bit *= 2
    return out


def kernel(
    n_blk,
    n_head,
    x_ref,
    lam_ref,
    gain_ref,
    out_ref,
    kv,
    q,
    m_ref,
    l_ref,
    acc,
    obuf,
    send_kv,
    recv_kv,
    send_q,
    recv_q,
    send_o,
    recv_o,
):
    b = lax.axis_index("blk")
    h = lax.axis_index("head")
    tok = x_ref.shape[1]
    heads_here = q.shape[0]
    kd = lam_ref.shape[1]
    vd = gain_ref.shape[1]
    kvw = 2 * kd + vd
    rows_half = tok * n_head // 2
    subs = n_head // 2
    bits = [1 << i for i in range(n_blk.bit_length() - 1)]
    plane = bits[1:]
    orders = [
        (plane if hh % 2 == 0 else plane[::-1]) + bits[:1] for hh in range(heads_here)
    ]

    barrier = pltpu.get_barrier_semaphore()
    partners = [(b, flip(h, j)) for j in range(1, n_head)]
    partners += [(flip(b, bit), h) for bit in bits]
    for partner in partners:
        pl.semaphore_signal(barrier, inc=1, device_id=partner, device_id_type=MESH)
    pl.semaphore_wait(barrier, len(partners))

    def slot(hh, code, src):
        return kv.at[
            hh, src // subs, code, pl.ds(pl.multiple_of((src % subs) * tok, tok), tok), :
        ]

    def last_step(code, hh):
        return max(i for i, bit in enumerate(orders[hh]) if code & bit)

    def x_kv(head):
        return x_ref.at[head, :, pl.ds(2 * kd, kvw)]

    def head_copy(j, hh):
        dest = flip(h, j)
        return pltpu.make_async_remote_copy(
            src_ref=x_kv(dest * heads_here + hh),
            dst_ref=slot(hh, 0, h),
            send_sem=send_kv.at[0, j, hh],
            recv_sem=recv_kv.at[0, j, hh],
            device_id=(b, dest),
            device_id_type=MESH,
        )

    def q_rows(src):
        return q.at[:, pl.ds(pl.multiple_of(src * tok, tok), tok), :]

    def x_q(dest):
        return x_ref.at[pl.ds(dest * heads_here, heads_here), :, pl.ds(0, 2 * kd)]

    def q_copy(j):
        dest = flip(h, j)
        return pltpu.make_async_remote_copy(
            src_ref=x_q(dest),
            dst_ref=q_rows(h),
            send_sem=send_q.at[j],
            recv_sem=recv_q.at[j],
            device_id=(b, dest),
            device_id_type=MESH,
        )

    def own_copy(hh):
        return pltpu.make_async_copy(
            x_kv(h * heads_here + hh), slot(hh, 0, h), recv_kv.at[0, 0, hh]
        )

    def own_q():
        return pltpu.make_async_copy(x_q(h), q_rows(h), recv_q.at[0])

    def blk_copy(code, j, hh):
        bit = orders[hh][last_step(code, hh)]
        before = code ^ bit
        src = flip(h, j)
        if before == 0 and j == 0:
            source = x_kv(h * heads_here + hh)
        else:
            source = slot(hh, before, src)
        return pltpu.make_async_remote_copy(
            src_ref=source,
            dst_ref=slot(hh, code, src),
            send_sem=send_kv.at[code, j, hh],
            recv_sem=recv_kv.at[code, j, hh],
            device_id=(flip(b, bit), h),
            device_id_type=MESH,
        )

    arrived = set()

    def arrive(code, j, hh):
        if (code, j, hh) in arrived:
            return
        arrived.add((code, j, hh))
        if code == 0 and j == 0:
            pass
        elif code == 0:
            head_copy(j, hh).wait_recv()
        else:
            blk_copy(code, j, hh).wait_recv()
        first = 0 if code == 0 else last_step(code, hh) + 1
        for bit in orders[hh][first:]:
            blk_copy(code ^ bit, j, hh).start()

    def spread(step, j):
        for hh in range(heads_here):
            if step < 0:
                arrive(0, j, hh)
            else:
                for code in range(1, n_blk):
                    if last_step(code, hh) == step:
                        arrive(code, j, hh)

    steps = len(bits)

    for hh in range(heads_here):
        own_copy(hh).start()
    own_q().start()
    for hh in range(heads_here):
        head_copy(1, hh).start()
    for j in range(n_head - 1, 0, -1):
        q_copy(j).start()
    for j in range(2, n_head):
        for hh in range(heads_here):
            head_copy(j, hh).start()
    spread(-1, 0)

    m_ref[...] = jnp.full(m_ref.shape, far_below, jnp.float32)
    l_ref[...] = jnp.zeros(l_ref.shape, jnp.float32)
    acc[...] = jnp.zeros(acc.shape, jnp.float32)

    rate = math.log2(math.e) / math.sqrt(kd)
    chip = b // 2

    def unit(half, g, js):
        for hh in range(heads_here):
            for code in (2 * g, 2 * g + 1):
                for j in js:
                    arrive(code, j, hh)
        if g == 0:
            low = half
        else:
            top = 1 << (g.bit_length() - 1)
            later = 1 - (chip // top) % 2
            low = later + (1 - later) * 2 * half

        def one(hh, qt):
            rows = pl.ds(pl.multiple_of(qt * rows_half, rows_half), rows_half)
            values = kv[hh, half, 2 * g : 2 * g + 2, :, 2 * kd :].reshape(2 * rows_half, vd)
            for mp in range(2):
                queries = q[hh, rows, mp * kd : (mp + 1) * kd]
                keys = kv[hh, half, 2 * g : 2 * g + 2, :, mp * kd : (mp + 1) * kd]
                scores = lax.dot_general(
                    queries,
                    keys.reshape(2 * rows_half, kd),
                    (((1,), (1,)), ((), ())),
                    preferred_element_type=jnp.float32,
                )
                if g == 0:
                    row = lax.broadcasted_iota(jnp.int32, scores.shape, 0)
                    col = lax.broadcasted_iota(jnp.int32, scores.shape, 1)
                    sib = half + (1 - 2 * half) * (b % 2)
                    reach = qt * (1 - half) * 2 * rows_half
                    seen = (col <= row + reach) | (col >= 2 * rows_half - sib * rows_half)
                    scores = jnp.where(seen, scores, far_below)
                m_old = m_ref[hh, mp, rows]
                m_new = jnp.maximum(m_old, jnp.max(scores, axis=1, keepdims=True))
                weights = jnp.exp2((scores - m_new) * rate)
                factor = jnp.exp2((m_old - m_new) * rate)
                m_ref[hh, mp, rows] = m_new
                l_ref[hh, mp, rows] = l_ref[hh, mp, rows] * factor + jnp.sum(
                    weights, axis=1, keepdims=True
                )
                acc[hh, mp, rows] = acc[hh, mp, rows] * factor + jnp.dot(
                    weights.astype(jnp.bfloat16), values, preferred_element_type=jnp.float32
                )

        def over_rows(qt, carry):
            lax.fori_loop(0, heads_here, lambda hh, c: (one(hh, qt), c)[1], 0)
            return carry

        lax.fori_loop(low, 2, over_rows, 0)

    groups = n_blk // 2
    early = h // subs
    late = 1 - early
    near = list(range(subs))
    far = list(range(subs, n_head))

    for j in near[1:]:
        spread(-1, j)
    for j in near:
        for step in range(steps - 1):
            spread(step, j)
    for hh in range(heads_here):
        own_copy(hh).wait()
    own_q().wait()
    for j in range(1, n_head):
        q_copy(j).wait_recv()
    unit(early, 0, near)
    todo = [(step, far[0]) for step in range(-1, steps - 1)]
    for g in range(1, groups):
        if todo:
            spread(*todo.pop(0))
        unit(early, g, near)
    for item in todo:
        spread(*item)
    for j in far[1:]:
        spread(-1, j)
    unit(late, 0, far)
    for j in far[1:]:
        for step in range(steps - 1):
            spread(step, j)
    for g in range(1, groups):
        unit(late, g, far)

    lam = (
        jnp.exp(jnp.sum(lam_ref[0:1, :] * lam_ref[1:2, :], axis=1, keepdims=True))
        - jnp.exp(jnp.sum(lam_ref[2:3, :] * lam_ref[3:4, :], axis=1, keepdims=True))
        + lambda_init
    )
    gain = gain_ref[...] * (1.0 - lambda_init)

    def finish(src):
        rows = pl.ds(pl.multiple_of(src * tok, tok), tok)
        for hh in range(heads_here):
            one_out = acc[hh, 0, rows] * (1.0 / l_ref[hh, 0, rows])
            two_out = acc[hh, 1, rows] * (lam / l_ref[hh, 1, rows])
            difference = one_out - two_out
            mean_square = jnp.mean(difference * difference, axis=1, keepdims=True)
            obuf[rows, hh * vd : (hh + 1) * vd] = (
                difference * lax.rsqrt(mean_square + 1e-05) * gain
            ).astype(jnp.bfloat16)

    width = heads_here * vd

    def place(owner):
        return out_ref.at[:, pl.ds(pl.multiple_of(owner * width, width), width)]

    def out_rows(src):
        return obuf.at[pl.ds(pl.multiple_of(src * tok, tok), tok), :]

    def out_copy(j):
        dest = flip(h, j)
        return pltpu.make_async_remote_copy(
            src_ref=out_rows(dest),
            dst_ref=place(h),
            send_sem=send_o.at[j],
            recv_sem=recv_o.at[j],
            device_id=(b, dest),
            device_id_type=MESH,
        )

    for j in range(n_head - 1, 0, -1):
        finish(flip(h, j))
        out_copy(j).start()
    finish(h)
    own_out = pltpu.make_async_copy(out_rows(h), place(h), recv_o.at[0])
    own_out.start()
    own_out.wait()

    for j in range(1, n_head):
        q_copy(j).wait_send()
        for hh in range(heads_here):
            head_copy(j, hh).wait_send()
    for j in range(n_head):
        for hh in range(heads_here):
            for code in range(1, n_blk):
                blk_copy(code, j, hh).wait_send()
    for j in range(1, n_head):
        out_copy(j).wait()


def local(n_blk, n_head, qkv, lambda_params, norm_gain):
    tok, heads, lanes = qkv.shape
    kd = lambda_params.shape[1]
    vd = norm_gain.shape[0]
    heads_here = heads // n_head
    rows = tok * n_head
    by_head = jnp.transpose(qkv, (1, 0, 2))
    return pl.pallas_call(
        functools.partial(kernel, n_blk, n_head),
        out_shape=jax.ShapeDtypeStruct((tok, heads * vd), jnp.bfloat16),
        in_specs=[
            pl.BlockSpec(memory_space=pl.ANY),
            pl.BlockSpec(memory_space=pltpu.VMEM),
            pl.BlockSpec(memory_space=pltpu.VMEM),
        ],
        out_specs=pl.BlockSpec(memory_space=pl.ANY),
        scratch_shapes=[
            pltpu.VMEM((heads_here, 2, n_blk, rows // 2, 2 * kd + vd), jnp.bfloat16),
            pltpu.VMEM((heads_here, rows, 2 * kd), jnp.bfloat16),
            pltpu.VMEM((heads_here, 2, rows, 1), jnp.float32),
            pltpu.VMEM((heads_here, 2, rows, 1), jnp.float32),
            pltpu.VMEM((heads_here, 2, rows, vd), jnp.float32),
            pltpu.VMEM((rows, heads_here * vd), jnp.bfloat16),
            pltpu.SemaphoreType.DMA((n_blk, n_head, heads_here)),
            pltpu.SemaphoreType.DMA((n_blk, n_head, heads_here)),
            pltpu.SemaphoreType.DMA((n_head,)),
            pltpu.SemaphoreType.DMA((n_head,)),
            pltpu.SemaphoreType.DMA((n_head,)),
            pltpu.SemaphoreType.DMA((n_head,)),
        ],
        compiler_params=pltpu.CompilerParams(
            collective_id=0, has_side_effects=True, vmem_limit_bytes=56 * 1024 * 1024
        ),
    )(by_head, lambda_params, norm_gain.reshape(1, vd))


def solution(mesh):
    n_blk, n_head = mesh.shape["blk"], mesh.shape["head"]
    return jax.shard_map(
        functools.partial(local, n_blk, n_head),
        mesh=mesh,
        in_specs=(P(("blk", "head"), None, None), P(), P()),
        out_specs=P(("blk", "head"), None),
        check_vma=False,
    )
```

time: 220 us -> 84.3 us (0.38)
  Pallas kernels: 0 us -> 78.9 us
  blocking collectives: 62.4 us -> 0 us
  waiting for transfers between devices: 50.8 us -> 0 us
  matrix products: 43.5 us -> 0 us
  other arithmetic: 24.5 us -> 0 us
  local copies, waits for them, and re-layouts: 23.7 us -> 4.73 us
  between operations: 14.9 us -> 0.01 us
    pallas_call x0 -> x1, Pallas kernels: none -> 78.9 us  [local(): pl.pallas_call(functools.partial(kernel, n_blk, n_head), out_shape=jax.Sh...]
    all_to_all x2 -> x0, blocking collectives: 62.4 us -> none  [the longest x1 43.1 us: local(): lax.all_to_all(qkv, 'head', split_axis=1, concat_axis=0, tiled=True)]
    all_gather x1 -> x0, waiting for transfers between devices: 50.8 us -> none  [local(): lax.all_gather(regrouped[:, :, 2 * key_width:], 'blk', axis=0, tiled=True)]
    dot_general x8 -> x0, matrix products: 43.5 us -> none  [the longest x4 22.6 us: update(): jnp.einsum('qhd,khd->hqk', queries, key_map, preferred_element_type=jnp.f...]
    reduce_sum x6 -> x0, other arithmetic: 20.9 us -> none  [the longest x4 18.3 us: update(): totals = totals * factor + jnp.sum(weights, axis=2)]
    while x28 -> x0, local copies, waits for them, and re-layouts: 9.75 us -> none
    slice x5 -> x0, local copies, waits for them, and re-layouts: 6.16 us -> none  [the longest x2 2.19 us: local(): values_all = pieces[:, :, 2 * key_width:]]
    le x4 -> x0, other arithmetic: 3.05 us -> none  [update(): visible = (key_pos[None, :] <= query_pos[:, None])[None, :, :]]
  transfers between devices with their start and end apart: 1 -> 0, of which waited for: 1 -> 0; matrix products, arithmetic and copies ran while one was open for 1% -> 0% of each run, Pallas kernels for 0% -> 0%
where the time goes in v1:
time: 84.3 us; the launch traced here: 83.7 us
  Pallas kernels  78.9 us (94%)
  local copies, waits for them, and re-layouts  4.73 us (6%)
    pallas_call x1, Pallas kernels, local(): pl.pallas_call(functools.partial(kernel, n_blk, n_head), out_shape=jax.Sh...  78.9 us
    unnamed x2, local copies, waits for them, and re-layouts  4.73 us

profile of v1, /device:TPU:0, one launch (start us, length us, event | category | flops | bytes accessed | tf_op | source)
XLA Modules:
  0.0 83.7 jit_solution(5108268442804103048)
XLA Ops:
  0.0 2.9 %copy.6 = bf16[128,8,768]{2,0,1:T(8,128)(2,1)} copy(bf16[128,8,768]{2,1,0:T(8,128)(2,1)} %param.3) | data formatting | bytes 3145728 | tf_op args[0]
  2.9 78.9 %shard_map.37 = bf16[128,2048]{1,0:T(8,128)(2,1)} custom-call(bf16[8,128,768]{2,1,0:T(8,128)(2,1)} %bitcast.4, f32[4,128]{1,0:T(4,128)} %lam_ref.1, f32[1,256]{1,0:T(1,128)} %bitcast.5), custom_call_target="tpu_custom_call" | custom-call | tf_op jit(solution)/shard_map/pallas_call | solution.py:324
  81.8 1.9 %copy.8 = bf16[128,2048]{1,0:T(8,128)(2,1)} copy(bf16[128,2048]{1,0:T(8,128)(2,1)} %shard_map.37) | data formatting | bytes 1048576

commit v2 on v1

v2 whole, which is shorter than its diff:
```python
import functools
import math

import jax
import jax.numpy as jnp
from jax import lax
from jax.experimental import pallas as pl
from jax.experimental.pallas import tpu as pltpu
from jax.sharding import PartitionSpec as P

lambda_init = 0.2
far_below = -1e30
MESH = pl.DeviceIdType.MESH


def flip(index, code):
    out = index
    bit = 1
    while bit <= code:
        if code & bit:
            out = out + (1 - 2 * ((index // bit) % 2)) * bit
        bit *= 2
    return out


def kernel(
    n_blk,
    n_head,
    x_ref,
    lam_ref,
    gain_ref,
    out_ref,
    kv,
    q,
    m_ref,
    l_ref,
    acc,
    obuf,
    send_kv,
    recv_kv,
    send_q,
    recv_q,
    send_o,
    recv_o,
):
    b = lax.axis_index("blk")
    h = lax.axis_index("head")
    tok = x_ref.shape[1]
    heads_here = q.shape[0]
    kd = lam_ref.shape[1]
    vd = gain_ref.shape[1]
    kvw = 2 * kd + vd
    rows_half = tok * n_head // 2
    subs = n_head // 2
    bits = [1 << i for i in range(n_blk.bit_length() - 1)]
    plane = bits[1:]
    orders = [plane + bits[:1], plane[::-1] + bits[:1]]

    barrier = pltpu.get_barrier_semaphore()
    partners = [(b, flip(h, j)) for j in range(1, n_head)]
    partners += [(flip(b, bit), h) for bit in bits]
    for partner in partners:
        pl.semaphore_signal(barrier, inc=1, device_id=partner, device_id_type=MESH)
    pl.semaphore_wait(barrier, len(partners))

    def slot(hh, code, src):
        return kv.at[
            hh, src // subs, code, pl.ds(pl.multiple_of((src % subs) * tok, tok), tok), :
        ]

    def last_step(code, way):
        return max(i for i, bit in enumerate(orders[way]) if code & bit)

    def x_kv(head):
        return x_ref.at[head, :, pl.ds(2 * kd, kvw)]

    def head_copy(j, hh):
        dest = flip(h, j)
        return pltpu.make_async_remote_copy(
            src_ref=x_kv(dest * heads_here + hh),
            dst_ref=slot(hh, 0, h),
            send_sem=send_kv.at[0, j, hh],
            recv_sem=recv_kv.at[0, j, hh],
            device_id=(b, dest),
            device_id_type=MESH,
        )

    def q_rows(src):
        return q.at[:, pl.ds(pl.multiple_of(src * tok, tok), tok), :]

    def x_q(dest):
        return x_ref.at[pl.ds(dest * heads_here, heads_here), :, pl.ds(0, 2 * kd)]

    def q_copy(j):
        dest = flip(h, j)
        return pltpu.make_async_remote_copy(
            src_ref=x_q(dest),
            dst_ref=q_rows(h),
            send_sem=send_q.at[j],
            recv_sem=recv_q.at[j],
            device_id=(b, dest),
            device_id_type=MESH,
        )

    def own_copy(hh):
        return pltpu.make_async_copy(
            x_kv(h * heads_here + hh), slot(hh, 0, h), recv_kv.at[0, 0, hh]
        )

    def own_q():
        return pltpu.make_async_copy(x_q(h), q_rows(h), recv_q.at[0])

    def blk_copy(code, j, hh):
        way = (hh + j) % 2
        bit = orders[way][last_step(code, way)]
        before = code ^ bit
        src = flip(h, j)
        if before == 0 and j == 0:
            source = x_kv(h * heads_here + hh)
        else:
            source = slot(hh, before, src)
        return pltpu.make_async_remote_copy(
            src_ref=source,
            dst_ref=slot(hh, code, src),
            send_sem=send_kv.at[code, j, hh],
            recv_sem=recv_kv.at[code, j, hh],
            device_id=(flip(b, bit), h),
            device_id_type=MESH,
        )

    steps = len(bits)
    near = list(range(subs))
    far = list(range(subs, n_head))
    heads = list(range(heads_here))

    def arrive(arrived, code, j, hh):
        if (code, j, hh) in arrived:
            return
        arrived.add((code, j, hh))
        way = (hh + j) % 2
        if code == 0 and j:
            head_copy(j, hh).wait_recv()
        elif code:
            blk_copy(code, j, hh).wait_recv()
        first = 0 if code == 0 else last_step(code, way) + 1
        for bit in orders[way][first:]:
            blk_copy(code ^ bit, j, hh).start()

    def spread(arrived, step, js, hhs):
        for j in js:
            for hh in hhs:
                if step < 0:
                    arrive(arrived, 0, j, hh)
                    continue
                for code in range(1, n_blk):
                    if last_step(code, (hh + j) % 2) == step:
                        arrive(arrived, code, j, hh)

    def inner(arrived, js, hhs, first=0):
        for step in range(first, steps - 1):
            spread(arrived, step, js, hhs)

    far_keys = [head_copy(j, hh) for hh in heads for j in far]
    far_queries = [q_copy(j) for j in far]
    queue_low = far_keys + far_queries
    queue_high = far_queries + far_keys
    third = len(queue_low) // 3
    cuts = [0, third + third // 2, 2 * third + third // 2, len(queue_low)]

    def send(queue, stage):
        for copy in queue[cuts[stage] : cuts[stage + 1]]:
            copy.start()

    for hh in heads:
        own_copy(hh).start()
    own_q().start()
    for j in near[1:]:
        for hh in heads:
            head_copy(j, hh).start()
    pl.when(h < subs)(functools.partial(send, queue_low, 0))
    pl.when(h >= subs)(functools.partial(send, queue_high, 0))
    for j in near[1:]:
        q_copy(j).start()
    sent_own = set()
    spread(sent_own, -1, [0], heads)

    m_ref[...] = jnp.full(m_ref.shape, far_below, jnp.float32)
    l_ref[...] = jnp.zeros(l_ref.shape, jnp.float32)
    acc[...] = jnp.zeros(acc.shape, jnp.float32)

    rate = math.log2(math.e) / math.sqrt(kd)
    chip = b // 2

    def one(half, g, hh, qt):
        rows = pl.ds(pl.multiple_of(qt * rows_half, rows_half), rows_half)
        values = kv[hh, half, pl.ds(2 * g, 2), :, 2 * kd :].reshape(2 * rows_half, vd)
        for mp in range(2):
            queries = q[hh, rows, mp * kd : (mp + 1) * kd]
            keys = kv[hh, half, pl.ds(2 * g, 2), :, mp * kd : (mp + 1) * kd]
            scores = lax.dot_general(
                queries,
                keys.reshape(2 * rows_half, kd),
                (((1,), (1,)), ((), ())),
                preferred_element_type=jnp.float32,
            )
            if isinstance(g, int) and g == 0:
                row = lax.broadcasted_iota(jnp.int32, scores.shape, 0)
                col = lax.broadcasted_iota(jnp.int32, scores.shape, 1)
                sib = half + (1 - 2 * half) * (b % 2)
                reach = qt * (1 - half) * 2 * rows_half
                seen = (col <= row + reach) | (col >= 2 * rows_half - sib * rows_half)
                scores = jnp.where(seen, scores, far_below)
            m_old = m_ref[hh, mp, rows]
            m_new = jnp.maximum(m_old, jnp.max(scores, axis=1, keepdims=True))
            weights = jnp.exp2((scores - m_new) * rate)
            factor = jnp.exp2((m_old - m_new) * rate)
            m_ref[hh, mp, rows] = m_new
            l_ref[hh, mp, rows] = l_ref[hh, mp, rows] * factor + jnp.sum(
                weights, axis=1, keepdims=True
            )
            acc[hh, mp, rows] = acc[hh, mp, rows] * factor + jnp.dot(
                weights.astype(jnp.bfloat16), values, preferred_element_type=jnp.float32
            )

    def lowest(half, g):
        if isinstance(g, int) and g == 0:
            return half
        later = 1 - (chip % 2)
        for top in [1 << i for i in range(1, groups.bit_length() - 1)]:
            later = jnp.where(g >= top, 1 - (chip // top) % 2, later)
        return later + (1 - later) * 2 * half

    groups = n_blk // 2
    chunks = [[0]]
    if groups <= 4:
        chunks += [[g] for g in range(1, groups)]
    else:
        chunks += [list(range(1, groups))]

    def work(arrived, half, chunk, hhs, js, qts):
        for hh in hhs:
            for g in chunk:
                for code in (2 * g, 2 * g + 1):
                    for j in js:
                        arrive(arrived, code, j, hh)

        def group(g):
            low = lowest(half, g)
            if qts == [1]:
                begin, end = jnp.maximum(low, 1), 2
            elif qts == [0]:
                begin, end = jnp.minimum(low, 1), 1
            else:
                begin, end = low, 2

            def row(qt, c):
                for hh in hhs:
                    one(half, g, hh, qt)
                return c

            lax.fori_loop(begin, end, row, 0)

        if len(chunk) == 1:
            group(chunk[0])
        else:
            lax.fori_loop(chunk[0], chunk[-1] + 1, lambda g, c: (group(g), c)[1], 0)

    lam = (
        jnp.exp(jnp.sum(lam_ref[0:1, :] * lam_ref[1:2, :], axis=1, keepdims=True))
        - jnp.exp(jnp.sum(lam_ref[2:3, :] * lam_ref[3:4, :], axis=1, keepdims=True))
        + lambda_init
    )
    gain = gain_ref[...] * (1.0 - lambda_init)

    def finish(hh, src):
        rows = pl.ds(pl.multiple_of(src * tok, tok), tok)
        one_out = acc[hh, 0, rows] * (1.0 / l_ref[hh, 0, rows])
        two_out = acc[hh, 1, rows] * (lam / l_ref[hh, 1, rows])
        difference = one_out - two_out
        mean_square = jnp.mean(difference * difference, axis=1, keepdims=True)
        obuf[rows, hh * vd : (hh + 1) * vd] = (
            difference * lax.rsqrt(mean_square + 1e-05) * gain
        ).astype(jnp.bfloat16)

    def place(owner, hh):
        return out_ref.at[:, pl.ds(pl.multiple_of((owner * heads_here + hh) * vd, vd), vd)]

    def out_rows(src, hh):
        return obuf.at[pl.ds(pl.multiple_of(src * tok, tok), tok), pl.ds(hh * vd, vd)]

    def out_copy(j, hh):
        dest = flip(h, j)
        return pltpu.make_async_remote_copy(
            src_ref=out_rows(dest, hh),
            dst_ref=place(h, hh),
            send_sem=send_o.at[j, hh],
            recv_sem=recv_o.at[j, hh],
            device_id=(b, dest),
            device_id_type=MESH,
        )

    def own_out(hh):
        return pltpu.make_async_copy(out_rows(h, hh), place(h, hh), recv_o.at[0, hh])

    def give(hh, js):
        for j in js:
            finish(hh, flip(h, j))
            (out_copy(j, hh) if j else own_out(hh)).start()

    def own_in():
        own_q().wait()
        for j in near[1:]:
            q_copy(j).wait_recv()
        for hh in heads:
            own_copy(hh).wait()

    def far_q_in():
        for j in far:
            q_copy(j).wait_recv()

    homeward = near[1:] + near[:1]

    def lower():
        got = set(sent_own)
        spread(got, -1, near[1:], heads)
        inner(got, near[:1], heads)
        spread(got, 0, near[1:], heads)
        far_q_in()
        send(queue_low, 1)
        inner(got, near[1:], heads, 1)
        own_in()
        work(got, 0, chunks[0], heads, near, [0, 1])
        for i, chunk in enumerate(chunks[1:]):
            work(got, 0, chunk, heads, near, [0, 1])
            if i == 0:
                spread(got, -1, far, heads[:1])
                send(queue_low, 2)
            if i == 1:
                spread(got, 0, far, heads[:1])
        inner(got, far, heads[:1])
        for hh in heads:
            rest = heads[hh + 1 : hh + 2]
            work(got, 1, chunks[0], [hh], far, [1])
            spread(got, -1, far, rest)
            for chunk in chunks[1:]:
                work(got, 1, chunk, [hh], far, [1])
            spread(got, 0, far, rest)
            give(hh, far)
            inner(got, far, rest, 1)
        for hh in heads:
            give(hh, homeward)

    def upper():
        got = set(sent_own)
        spread(got, -1, near[1:], heads)
        inner(got, near[:1], heads)
        spread(got, -1, far, heads[:1])
        send(queue_high, 1)
        spread(got, 0, near[1:], heads)
        spread(got, 0, far, heads[:1])
        inner(got, near[1:], heads, 1)
        own_in()
        work(got, 1, chunks[0], heads, near, [1])
        inner(got, far, heads[:1], 1)
        for chunk in chunks[1:]:
            work(got, 1, chunk, heads, near, [1])
        for hh in heads:
            rest = heads[hh + 1 : hh + 2]
            work(got, 0, chunks[0], [hh], far, [1])
            spread(got, -1, far, rest)
            if rest:
                send(queue_high, 2)
            for i, chunk in enumerate(chunks[1:]):
                work(got, 0, chunk, [hh], far, [1])
                if i == 0:
                    spread(got, 0, far, rest)
            inner(got, far, rest, 1)
        far_q_in()
        for hh in heads:
            for chunk in chunks:
                work(got, 0, chunk, [hh], far, [0])
            give(hh, far)
        for hh in heads:
            give(hh, homeward)

    pl.when(h < subs)(lower)
    pl.when(h >= subs)(upper)

    for hh in range(heads_here):
        own_out(hh).wait()
    for j in range(1, n_head):
        q_copy(j).wait_send()
        for hh in range(heads_here):
            head_copy(j, hh).wait_send()
    for j in range(n_head):
        for hh in range(heads_here):
            for code in range(1, n_blk):
                blk_copy(code, j, hh).wait_send()
    for j in range(1, n_head):
        for hh in range(heads_here):
            out_copy(j, hh).wait()


def local(n_blk, n_head, qkv, lambda_params, norm_gain):
    tok, heads, lanes = qkv.shape
    kd = lambda_params.shape[1]
    vd = norm_gain.shape[0]
    heads_here = heads // n_head
    rows = tok * n_head
    by_head = jnp.transpose(qkv, (1, 0, 2))
    return pl.pallas_call(
        functools.partial(kernel, n_blk, n_head),
        out_shape=jax.ShapeDtypeStruct((tok, heads * vd), jnp.bfloat16),
        in_specs=[
            pl.BlockSpec(memory_space=pl.ANY),
            pl.BlockSpec(memory_space=pltpu.VMEM),
            pl.BlockSpec(memory_space=pltpu.VMEM),
        ],
        out_specs=pl.BlockSpec(memory_space=pl.ANY),
        scratch_shapes=[
            pltpu.VMEM((heads_here, 2, n_blk, rows // 2, 2 * kd + vd), jnp.bfloat16),
            pltpu.VMEM((heads_here, rows, 2 * kd), jnp.bfloat16),
            pltpu.VMEM((heads_here, 2, rows, 1), jnp.float32),
            pltpu.VMEM((heads_here, 2, rows, 1), jnp.float32),
            pltpu.VMEM((heads_here, 2, rows, vd), jnp.float32),
            pltpu.VMEM((rows, heads_here * vd), jnp.bfloat16),
            pltpu.SemaphoreType.DMA((n_blk, n_head, heads_here)),
            pltpu.SemaphoreType.DMA((n_blk, n_head, heads_here)),
            pltpu.SemaphoreType.DMA((n_head,)),
            pltpu.SemaphoreType.DMA((n_head,)),
            pltpu.SemaphoreType.DMA((n_head, heads_here)),
            pltpu.SemaphoreType.DMA((n_head, heads_here)),
        ],
        compiler_params=pltpu.CompilerParams(
            collective_id=0, has_side_effects=True, vmem_limit_bytes=56 * 1024 * 1024
        ),
    )(by_head, lambda_params, norm_gain.reshape(1, vd))


def solution(mesh):
    n_blk, n_head = mesh.shape["blk"], mesh.shape["head"]
    return jax.shard_map(
        functools.partial(local, n_blk, n_head),
        mesh=mesh,
        in_specs=(P(("blk", "head"), None, None), P(), P()),
        out_specs=P(("blk", "head"), None),
        check_vma=False,
    )
```

time: 84.3 us -> 75.5 us (0.90)
  Pallas kernels: 78.9 us -> 69.7 us
    pallas_call x1, Pallas kernels: 78.9 us -> 69.7 us  [local(): pl.pallas_call(functools.partial(kernel, n_blk, n_head), out_shape=jax.Sh...]
where the time goes in v2:
time: 75.5 us; the launch traced here: 74.4 us
  Pallas kernels  69.7 us (92%)
  local copies, waits for them, and re-layouts  4.73 us (6%)
    pallas_call x1, Pallas kernels, local(): pl.pallas_call(functools.partial(kernel, n_blk, n_head), out_shape=jax.Sh...  69.7 us
    unnamed x2, local copies, waits for them, and re-layouts  4.73 us

profile of v2, /device:TPU:0, one launch (start us, length us, event | category | flops | bytes accessed | tf_op | source)
XLA Modules:
  0.0 74.4 jit_solution(8329801070839531833)
XLA Ops:
  0.0 2.9 %copy.6 = bf16[128,8,768]{2,0,1:T(8,128)(2,1)} copy(bf16[128,8,768]{2,1,0:T(8,128)(2,1)} %param.3) | data formatting | bytes 3145728 | tf_op args[0]
  2.9 69.7 %shard_map.37 = bf16[128,2048]{1,0:T(8,128)(2,1)} custom-call(bf16[8,128,768]{2,1,0:T(8,128)(2,1)} %bitcast.4, f32[4,128]{1,0:T(4,128)} %lam_ref.1, f32[1,256]{1,0:T(1,128)} %bitcast.5), custom_call_target="tpu_custom_call" | custom-call | tf_op jit(solution)/shard_map/pallas_call | solution.py:411
  72.5 1.9 %copy.8 = bf16[128,2048]{1,0:T(8,128)(2,1)} copy(bf16[128,2048]{1,0:T(8,128)(2,1)} %shard_map.37) | data formatting | bytes 1048576

commit v3 on v2

--- a/solution.py
+++ b/solution.py
@@ -165,7 +165,7 @@
     queue_low = far_keys + far_queries
     queue_high = far_queries + far_keys
     third = len(queue_low) // 3
-    cuts = [0, third + third // 2, 2 * third + third // 2, len(queue_low)]
+    cuts = [0, 2 * third] + [len(queue_low)] * 2
 
     def send(queue, stage):
         for copy in queue[cuts[stage] : cuts[stage + 1]]:

time: 75.5 us -> 75.7 us (level)
  no operation moved by 1% of the time
where the time goes in v3:
time: 75.7 us; the launch traced here: 74.7 us
  Pallas kernels  70 us (92%)
  local copies, waits for them, and re-layouts  4.73 us (6%)
    pallas_call x1, Pallas kernels, local(): pl.pallas_call(functools.partial(kernel, n_blk, n_head), out_shape=jax.Sh...  70 us
    unnamed x2, local copies, waits for them, and re-layouts  4.73 us

profile of v3, /device:TPU:0, one launch (start us, length us, event | category | flops | bytes accessed | tf_op | source)
XLA Modules:
  0.0 74.7 jit_solution(15018953506512104422)
XLA Ops:
  0.0 2.9 %copy.6 = bf16[128,8,768]{2,0,1:T(8,128)(2,1)} copy(bf16[128,8,768]{2,1,0:T(8,128)(2,1)} %param.3) | data formatting | bytes 3145728 | tf_op args[0]
  2.9 70.0 %shard_map.37 = bf16[128,2048]{1,0:T(8,128)(2,1)} custom-call(bf16[8,128,768]{2,1,0:T(8,128)(2,1)} %bitcast.4, f32[4,128]{1,0:T(4,128)} %lam_ref.1, f32[1,256]{1,0:T(1,128)} %bitcast.5), custom_call_target="tpu_custom_call" | custom-call | tf_op jit(solution)/shard_map/pallas_call | solution.py:411
  72.9 1.9 %copy.8 = bf16[128,2048]{1,0:T(8,128)(2,1)} copy(bf16[128,2048]{1,0:T(8,128)(2,1)} %shard_map.37) | data formatting | bytes 1048576
